TPU v7x, 128 devices: a whole 4x4x4 slice. The times are simulated.
128 devices in a mesh: shot: 8 (over z, y_lo), rcv: 16 (over y_hi, x, core).
Axes of the slice: x: 4, y: 4 (y_hi: 2, y_lo: 2; y = y_hi * 2 + y_lo), z: 4, core: 2. Of those that a mesh axis runs over, the one named last changes fastest.
Arguments:
- traces: bfloat16 [768, 768, 512], P('shot', 'rcv'), may hold values from -6 to 6
- source_weight: float32 [2, 256, 768], P(None, ('shot', 'rcv')), may hold values from -0.15625 to 0.15625
Outputs:
- multiples: bfloat16 [768, 768, 512], P('shot', 'rcv')
All inputs are finite; a program needn't handle non-finite values.
Results may differ from a plain program's by a relative error of at most 0.0092.
Values may be sent and summed in bfloat16 or wider, within the bound.
A program may use at most 128 MiB of HBM per device.

v0:
```python
import math

import jax
import jax.numpy as jnp
from jax import lax
from jax.sharding import PartitionSpec as P

STATIONS = 768
FREQS = 256


def dft_basis(count_freq, count_time):
    temporal_pitch = jnp.arange(count_freq, dtype=jnp.int32)
    moments = jnp.arange(count_time, dtype=jnp.int32)
    phase = (temporal_pitch[:, None] * moments[None, :] % count_time).astype(jnp.float32) * (
        2.0 * math.pi / count_time
    )
    stacked = jnp.stack([jnp.cos(phase), -jnp.sin(phase)], axis=1)
    return stacked.reshape(2 * count_freq, count_time).astype(jnp.bfloat16)


def predict_single(operands):
    one_slice, one_weight = operands
    summed = one_slice.astype(jnp.float32) + jnp.swapaxes(one_slice, 1, 2).astype(jnp.float32)
    averaged = (0.5 * summed).astype(jnp.bfloat16)
    average_inphase_part = averaged[0]
    average_quadrature_part = averaged[1]
    real_f32 = average_inphase_part.astype(jnp.float32)
    imag_f32 = average_quadrature_part.astype(jnp.float32)
    weight_real = one_weight[0][:, None]
    weight_imag = one_weight[1][:, None]
    emitter_scaled_inphase = (weight_real * real_f32 - weight_imag * imag_f32).astype(jnp.bfloat16)
    emitter_scaled_quadrature = (weight_real * imag_f32 + weight_imag * real_f32).astype(
        jnp.bfloat16
    )
    left_operand = jnp.concatenate([average_inphase_part, average_quadrature_part], axis=1)
    upper = jnp.concatenate([emitter_scaled_inphase, emitter_scaled_quadrature], axis=1)
    lower = jnp.concatenate([-emitter_scaled_quadrature, emitter_scaled_inphase], axis=1)
    second_factor = jnp.concatenate([upper, lower], axis=0)
    complex_product = jnp.dot(left_operand, second_factor, preferred_element_type=jnp.float32)
    order_rows, double_cols = complex_product.shape
    split_parts = complex_product.reshape(order_rows, 2, double_cols // 2)
    return split_parts.transpose(1, 0, 2).astype(jnp.bfloat16)


def predict_slices(slices, weights):
    return lax.map(predict_single, (slices, jnp.swapaxes(weights, 0, 1)))


def on_device(traces, source_weight):
    shot_dev, rcv_dev, samples = traces.shape
    stations = STATIONS
    frequencies = FREQS
    shot_count = lax.axis_size("shot")
    rcv_count = lax.axis_size("rcv")
    traces_local = shot_dev * rcv_dev
    freq_local = frequencies // (shot_count * rcv_count)
    basis = dft_basis(frequencies, samples)
    flattened = traces.reshape(traces_local, samples)
    spectra = lax.dot_general(
        basis, flattened, (((1,), (1,)), ((), ())), preferred_element_type=jnp.float32
    )
    spectra = (
        (spectra * samples ** (-0.5))
        .astype(jnp.bfloat16)
        .reshape(frequencies, 2, shot_dev, rcv_dev)
    )
    received = lax.all_to_all(spectra, ("shot", "rcv"), split_axis=0, concat_axis=3, tiled=True)
    received = received.reshape(freq_local, 2, shot_dev, shot_count, stations)
    slices = received.transpose(0, 1, 3, 2, 4).reshape(freq_local, 2, stations, stations)
    predicted = predict_slices(slices, source_weight)
    outgoing = predicted.reshape(freq_local, 2, shot_count, shot_dev, stations)
    outgoing = outgoing.transpose(0, 1, 3, 2, 4).reshape(
        freq_local, 2, shot_dev, shot_count * stations
    )
    returned = lax.all_to_all(outgoing, ("shot", "rcv"), split_axis=3, concat_axis=0, tiled=True)
    gathered = returned.reshape(2 * frequencies, traces_local)
    series = lax.dot_general(
        gathered, basis, (((0,), (0,)), ((), ())), preferred_element_type=jnp.float32
    )
    series = (series * (2.0 / samples) ** 0.5).astype(jnp.bfloat16)
    return series.reshape(shot_dev, rcv_dev, samples)


def solution(mesh):
    placed = (P("shot", "rcv", None), P(None, ("shot", "rcv"), None))
    return jax.shard_map(
        on_device, mesh=mesh, in_specs=placed, out_specs=P("shot", "rcv", None), check_vma=False
    )
```

profile of v0, /device:TPU:2, one launch (start us, length us, event | category | flops | bytes accessed | tf_op | source)
XLA Modules:
  0.0 344.0 jit_solution(5611496034216499578)
XLA Ops:
  3.0 6.8 %multiply_convert_fusion.1 = bf16[512,4608]{1,0:T(8,128)(2,1)} fusion(bf16[512,512]{1,0:T(8,128)(2,1)S(1)} %convert_element_type.74, bf16[4608,512]{1,0:T(8,128)(2,1)} %bitcast.76), kind=kOutput, calls=%fused_computation.31 | convolution fusion | flops 2420637696 | bytes 9961472 | tf_op jit(solution)/shard_map/dot_general | solution.py:60
  9.8 17.1 %reshape.120 = bf16[256,2,96,48]{3,2,1,0:T(8,128)(2,1)} reshape(bf16[512,4608]{1,0:T(8,128)(2,1)} %multiply_convert_fusion.1) | data formatting | bytes 9437184 | tf_op jit(solution)/shard_map/reshape | solution.py:66
  27.0 12.9 %copy.38 = bf16[256,2,96,48]{2,3,1,0:T(8,128)(2,1)} copy(bf16[256,2,96,48]{3,2,1,0:T(8,128)(2,1)} %reshape.120) | data formatting | bytes 9437184 | tf_op jit(solution)/shard_map/reshape | solution.py:66
  39.9 10.9 %all-to-all-start = ((bf16[256,2,96,48]{2,3,1,0:T(8,128)(2,1)}), bf16[256,2,96,48]{2,3,1,0:T(8,128)(2,1)}, u32[]{:S(2)}, u32[]{:S(2)}) async-start(bf16[256,2,96,48]{2,3,1,0:T(8,128)(2,1)} %copy.38), calls=%async_computation | async-start | bytes 12582912 | tf_op jit(solution)/shard_map/all_to_all | solution.py:68
  50.9 75.8 %all-to-all-done = bf16[256,2,96,48]{2,3,1,0:T(8,128)(2,1)} async-done(((bf16[256,2,96,48]{2,3,1,0:T(8,128)(2,1)}), bf16[256,2,96,48]{2,3,1,0:T(8,128)(2,1)}, u32[]{:S(2)}, u32[]{:S(2)}) %all-to-all-start) | async-done | bytes 4718624 | tf_op jit(solution)/shard_map/all_to_all | solution.py:68
  126.6 6.5 %copy.39 = bf16[128,2,2,96,48]{3,4,0,2,1:T(8,128)(2,1)} copy(bf16[128,2,2,96,48]{3,4,2,1,0:T(8,128)(2,1)} %bitcast.8) | data formatting | bytes 9437184 | tf_op jit(solution)/shard_map/all_to_all | solution.py:68
  133.1 8.0 %copy.40 = bf16[2,2,8,96,768]{4,3,2,1,0:T(8,128)(2,1)} copy(bf16[2,2,8,96,768]{3,4,2,1,0:T(8,128)(2,1)} %bitcast.70) | data formatting | bytes 9437184 | tf_op jit(solution)/shard_map/transpose | solution.py:70
  141.2 56.9 %while.10 = (s32[]{:T(128)}, bf16[2,2,768,768]{3,1,2,0:T(2,128)(2,1)}, bf16[2,2,768,768]{3,2,1,0:T(8,128)(2,1)}, f32[2,2,768]{2,1,0:T(2,128)S(1)}, s32[]{:T(128)}, /*index=5*/s32[]{:T(128)}, s32[]{}) while((s32[]{:T(128)}, bf16[2,2,768,768]{3,1,2,0:T(2,128)(2,1)}, bf16[2,2,768,768]{3,2,1,0:T(8,128)(2,1)}, f32[2,2,768]{2,1,0:T(2,128)S(1)}, ...), condition=%wide.region_1.2_spmd, body=%wide.region_0.1_spmd.sunk | while | flops 3662217216 | bytes 56648296 | solution.py:47
  141.2 4.2 %bitcast_convert_fusion.2 = f32[2,768,768]{2,1,0:T(8,128)} fusion(bf16[2,2,768,768]{3,2,1,0:T(8,128)(2,1)} %get-tuple-element.97, s32[]{:T(128)} %get-tuple-element.88), kind=kLoop, calls=%fused_computation.24.clone.2 | loop fusion | flops 1179648 | bytes 7077892 | tf_op jit(solution)/shard_map/while/body/eval_jaxpr/convert_element_type | solution.py:24
  145.4 6.0 %copy.52 = f32[2,768,768]{1,2,0:T(8,128)} copy(f32[2,768,768]{2,1,0:T(8,128)} %bitcast_convert_fusion.2) | data formatting | bytes 9437184 | tf_op jit(solution)/shard_map/while/body/eval_jaxpr/convert_element_type | solution.py:24
  151.4 3.7 %fusion.41 = bf16[2,768,768]{1,2,0:T(8,128)(2,1)S(1)} fusion(f32[2,768,768]{1,2,0:T(8,128)} %copy.52, bf16[2,2,768,768]{3,2,1,0:T(8,128)(2,1)} %get-tuple-element.97, s32[]{:T(128)} %get-tuple-element.88), kind=kLoop, calls=%fused_computation.10.clone.1 | loop fusion | flops 4718592 | bytes 9437188 | tf_op jit(solution)/shard_map/while/body/eval_jaxpr/convert_element_type | solution.py:25
  156.3 5.3 %fusion.44 = bf16[768,1536]{1,0:T(8,128)(2,1)} fusion(bf16[768,768]{0,1:T(8,128)(2,1)S(1)} %fusion.42, bf16[768,768]{0,1:T(8,128)(2,1)S(1)} %get-tuple-element.77, bf16[768,768]{0,1:T(8,128)(2,1)S(1)} %get-tuple-element.78, bf16[768,768]{0,1:T(8,128)(2,1)S(1)} %get-tuple-element.79, bf16[768,768]{0,1:T(8,128)(2,1)S(1)} %get-tuple-element.80), kind=kOutput, calls=%fused_computation.11.clone.1 | convolution fusion | flops 3648651264 | bytes 8257536 | tf_op jit(solution)/shard_map/while/body/eval_jaxpr/dot_general | solution.py:40
  161.6 5.0 %convert_element_type.123 = bf16[768,2,768]{2,1,0:T(2,128)(2,1)S(1)} reshape(bf16[768,1536]{1,0:T(8,128)(2,1)} %fusion.44) | data formatting | bytes 4718592 | tf_op jit(solution)/shard_map/while/body/eval_jaxpr/convert_element_type | solution.py:43
  169.6 4.2 %bitcast_convert_fusion.2 = f32[2,768,768]{2,1,0:T(8,128)} fusion(bf16[2,2,768,768]{3,2,1,0:T(8,128)(2,1)} %get-tuple-element.97, s32[]{:T(128)} %get-tuple-element.88), kind=kLoop, calls=%fused_computation.24.clone.2 | loop fusion | flops 1179648 | bytes 7077892 | tf_op jit(solution)/shard_map/while/body/eval_jaxpr/convert_element_type | solution.py:24
  173.8 6.0 %copy.52 = f32[2,768,768]{1,2,0:T(8,128)} copy(f32[2,768,768]{2,1,0:T(8,128)} %bitcast_convert_fusion.2) | data formatting | bytes 9437184 | tf_op jit(solution)/shard_map/while/body/eval_jaxpr/convert_element_type | solution.py:24
  179.8 3.7 %fusion.41 = bf16[2,768,768]{1,2,0:T(8,128)(2,1)S(1)} fusion(f32[2,768,768]{1,2,0:T(8,128)} %copy.52, bf16[2,2,768,768]{3,2,1,0:T(8,128)(2,1)} %get-tuple-element.97, s32[]{:T(128)} %get-tuple-element.88), kind=kLoop, calls=%fused_computation.10.clone.1 | loop fusion | flops 4718592 | bytes 9437188 | tf_op jit(solution)/shard_map/while/body/eval_jaxpr/convert_element_type | solution.py:25
  184.7 5.3 %fusion.44 = bf16[768,1536]{1,0:T(8,128)(2,1)} fusion(bf16[768,768]{0,1:T(8,128)(2,1)S(1)} %fusion.42, bf16[768,768]{0,1:T(8,128)(2,1)S(1)} %get-tuple-element.77, bf16[768,768]{0,1:T(8,128)(2,1)S(1)} %get-tuple-element.78, bf16[768,768]{0,1:T(8,128)(2,1)S(1)} %get-tuple-element.79, bf16[768,768]{0,1:T(8,128)(2,1)S(1)} %get-tuple-element.80), kind=kOutput, calls=%fused_computation.11.clone.1 | convolution fusion | flops 3648651264 | bytes 8257536 | tf_op jit(solution)/shard_map/while/body/eval_jaxpr/dot_general | solution.py:40
  190.0 5.0 %convert_element_type.123 = bf16[768,2,768]{2,1,0:T(2,128)(2,1)S(1)} reshape(bf16[768,1536]{1,0:T(8,128)(2,1)} %fusion.44) | data formatting | bytes 4718592 | tf_op jit(solution)/shard_map/while/body/eval_jaxpr/convert_element_type | solution.py:43
  198.0 7.2 %copy.49 = bf16[2,2,8,96,768]{4,2,3,1,0:T(8,128)(2,1)} copy(bf16[2,2,8,96,768]{4,1,3,2,0:T(2,128)(2,1)} %bitcast.74) | data formatting | bytes 9437184 | tf_op jit(solution)/shard_map/reshape | solution.py:72
  205.2 11.5 %copy.46 = bf16[2,2,96,8,768]{2,1,0,4,3:T(2,128)(2,1)} copy(bf16[2,2,96,8,768]{4,3,2,1,0:T(8,128)(2,1)} %bitcast.73) | data formatting | bytes 9437184 | tf_op jit(solution)/shard_map/reshape | solution.py:73
  216.8 80.6 %all_to_all.30 = bf16[2,2,96,6144]{2,1,0,3:T(2,128)(2,1)S(1)} all-to-all(bf16[2,2,96,6144]{2,1,0,3:T(2,128)(2,1)} %bitcast.71), channel_id=1, replica_groups=mesh['shot'=8,'rcv'=16] {'shot','rcv'}, dimensions={3} | all-to-all | bytes 9437184 | tf_op jit(solution)/shard_map/all_to_all | solution.py:76
  300.8 12.8 %copy.45 = bf16[128,2,2,96,48]{4,3,2,1,0:T(8,128)(2,1)} copy(bf16[128,2,2,96,48]{3,4,0,2,1:T(8,128)(2,1)} %bitcast.72) | data formatting | bytes 9437184 | tf_op jit(solution)/shard_map/all_to_all | solution.py:76
  313.6 23.8 %reshape.125 = bf16[512,4608]{1,0:T(8,128)(2,1)} reshape(bf16[128,2,2,96,48]{4,3,2,1,0:T(8,128)(2,1)} %copy.45) | data formatting | bytes 9437184 | tf_op jit(solution)/shard_map/reshape | solution.py:77
  337.3 6.6 %multiply_convert_fusion = bf16[4608,512]{1,0:T(8,128)(2,1)} fusion(bf16[512,4608]{1,0:T(8,128)(2,1)} %reshape.125, bf16[512,512]{1,0:T(8,128)(2,1)S(1)} %copy-done.1), kind=kOutput, calls=%fused_computation.30 | convolution fusion | flops 2420637696 | bytes 9961472 | tf_op jit(solution)/shard_map/dot_general | solution.py:78
  (23 shorter events, 14.8 us)
Async XLA Ops:
  3.0 6.8 %copy-start = (bf16[512,512]{1,0:T(8,128)(2,1)}, bf16[512,512]{1,0:T(8,128)(2,1)S(1)}, u32[]{:S(2)}) copy-start(bf16[512,512]{1,0:T(8,128)(2,1)S(1)} %convert_element_type.74) | copy-start | bytes 1572868
  39.9 11.0 %copy-start.2 = (f32[2,2,768]{2,1,0:T(2,128)S(1)}, f32[2,2,768]{2,1,0:T(2,128)}, u32[]{:S(2)}) copy-start(f32[2,2,768]{2,1,0:T(2,128)} %param.5) | copy-start | bytes 36868
  39.9 86.7 %all-to-all-start = ((bf16[256,2,96,48]{2,3,1,0:T(8,128)(2,1)}), bf16[256,2,96,48]{2,3,1,0:T(8,128)(2,1)}, u32[]{:S(2)}, u32[]{:S(2)}) async-start(bf16[256,2,96,48]{2,3,1,0:T(8,128)(2,1)} %copy.38), calls=%async_computation | async-start | bytes 12582912 | tf_op jit(solution)/shard_map/all_to_all | solution.py:68
  313.6 23.8 %copy-start.1 = (bf16[512,512]{1,0:T(8,128)(2,1)S(1)}, bf16[512,512]{1,0:T(8,128)(2,1)}, u32[]{:S(2)}) copy-start(bf16[512,512]{1,0:T(8,128)(2,1)} %copy-done) | copy-start | bytes 1572868
where the time goes:
time: 347 us; the launch traced here: 344 us
  local copies, waits for them, and re-layouts  132 us (38%)
  blocking collectives  80.6 us (23%)
  waiting for transfers between devices  75.8 us (22%)
  matrix products  24.1 us (7%)
  other arithmetic  20 us (6%)
  starting transfers between devices  10.9 us (3%)
    all_to_all x1, blocking collectives, on_device(): lax.all_to_all(outgoing, ('shot', 'rcv'), split_axis=3, concat_axis=0, ti...  80.6 us
    all_to_all x1, waiting for transfers between devices, on_device(): lax.all_to_all(spectra, ('shot', 'rcv'), split_axis=0, concat_axis=3, til...  75.8 us
    reshape x2, local copies, waits for them, and re-layouts, on_device(): spectra = (spectra * samples ** (-0.5)).astype(jnp.bfloat16).reshape(freq...  30.1 us
    reshape x1, local copies, waits for them, and re-layouts, on_device(): gathered = returned.reshape(2 * frequencies, traces_local)  23.8 us
    all_to_all x2, local copies, waits for them, and re-layouts, on_device(): lax.all_to_all(outgoing, ('shot', 'rcv'), split_axis=3, concat_axis=0, ti...  16.2 us
    convert_element_type x2, local copies, waits for them, and re-layouts, predict_single(): one_slice.astype(jnp.float32)  12.1 us
    reshape x1, local copies, waits for them, and re-layouts, on_device(): outgoing.transpose(0, 1, 3, 2, 4)  11.5 us
    all_to_all x1, starting transfers between devices, on_device(): lax.all_to_all(spectra, ('shot', 'rcv'), split_axis=0, concat_axis=3, til...  10.9 us
  transfers between devices with their start and end apart: 1, of which 1 were waited for; matrix products, arithmetic and copies ran while one was open for 0% of the time, Pallas kernels for 0%

commit v1 on v0

v1 whole, which is shorter than its diff:
```python
import functools
import math

import jax
import jax.numpy as jnp
import numpy as np
from jax import lax
from jax.experimental import pallas as pl
from jax.experimental.pallas import tpu as pltpu
from jax.sharding import PartitionSpec as P

MESH = pl.DeviceIdType.MESH
BF16, F32 = jnp.bfloat16, jnp.float32

STATIONS = 768
SAMPLES = 512
FREQS = 256
SHOTS = 8
RCVS = 16
DEVS = SHOTS * RCVS
HALF = 48
BAND = 16
BANDS = HALF // BAND
LANES = 128
TILES = 3
ROWS_MSG = TILES * BAND


def basis_table():
    freq = np.arange(FREQS)
    phase = ((freq[:, None] * np.arange(SAMPLES)[None, :]) % SAMPLES).astype(np.float32)
    phase = phase * np.float32(2.0 * math.pi / SAMPLES)
    rows = np.stack([np.cos(phase), -np.sin(phase)], axis=1).reshape(2 * FREQS, SAMPLES)
    rows = rows.reshape(DEVS, 4, SAMPLES).transpose(1, 0, 2).reshape(2 * FREQS, SAMPLES)
    return jnp.asarray(rows.astype(jnp.bfloat16))


def lane_of(rows):
    return lax.broadcasted_iota(jnp.int32, (rows, LANES), 1)


def turned(tile, amount):
    amount %= LANES
    return tile if amount == 0 else pltpu.roll(tile, amount, 1)


def peer(step):
    v = (step * 63) % DEVS
    bits = [(v // (1 << b)) % 2 for b in range(7)]
    dx, dy, dz, dc = 2 * bits[0] + bits[5], 2 * bits[1] + bits[2], 2 * bits[6] + bits[4], bits[3]
    shot, rcv = lax.axis_index("shot"), lax.axis_index("rcv")
    x = ((rcv // 2) % 4 + dx) % 4
    y = ((rcv // 8) * 2 + shot % 2 + dy) % 4
    z = (shot // 2 + dz) % 4
    c = (rcv % 2 + dc) % 2
    return z * 2 + y % 2, (y // 2) * 8 + x * 2 + c


def predict_kernel(
    x_hbm, basis, weight, back, xbuf, fbuf, s1, r1, mbuf, abuf, lbuf, pbuf, s2,
    xsem, send_sem, recv_sem,
):
    shot, rcv = lax.axis_index("shot"), lax.axis_index("rcv")
    me = shot * RCVS + rcv

    def greet(step, carry):
        pl.semaphore_signal(
            pltpu.get_barrier_semaphore(), inc=1, device_id=peer(step), device_id_type=MESH
        )
        return carry

    def x_copy(ts):
        band = pl.ds(ts * BAND, BAND)
        return pltpu.make_async_copy(x_hbm.at[:, band], xbuf.at[:, band], xsem.at[ts])

    for ts in range(BANDS):
        x_copy(ts).start()
    lax.fori_loop(1, DEVS, greet, 0)

    def transform(ts):
        def pair(u, carry):
            rhs = []
            for e in range(2):
                s = ts * BAND + 2 * u + e
                first = xbuf[0, s]
                rhs += [first, xbuf[1, s], first[:32]]
            z = lax.dot_general(
                basis[...], jnp.concatenate(rhs, 0), (((1,), (1,)), ((), ())),
                preferred_element_type=F32,
            )
            lane = lane_of(DEVS)
            for e in range(2):
                zq = [
                    turned(z[q * DEVS : (q + 1) * DEVS, e * LANES : (e + 1) * LANES], 96 * q)
                    for q in range(4)
                ]
                for k in range(TILES):
                    tile = jnp.where(lane < 96 - 32 * k, zq[k], zq[k + 1])
                    fbuf[pl.ds(k * BAND + 2 * u + e, DEVS, stride=ROWS_MSG), :] = (
                        tile * SAMPLES ** (-0.5)
                    )
            return carry

        lax.fori_loop(0, BAND // 2, pair, 0)

        def narrow(g, carry):
            rows = fbuf[pl.ds(pl.multiple_of(g * 8 * ROWS_MSG, 8 * ROWS_MSG), 8 * ROWS_MSG), :]
            s1[pl.ds(g * 8, 8), ts] = rows.astype(BF16).reshape(8, TILES, BAND, LANES)
            return carry

        lax.fori_loop(0, DEVS // 8, narrow, 0)

    def send_all(cut_src, cut_dst, n):
        local = pltpu.make_async_copy(cut_src(me), cut_dst(me), recv_sem.at[n])
        local.start()

        def send(step, carry):
            ps, pr = peer(step)
            pltpu.make_async_remote_copy(
                src_ref=cut_src(ps * RCVS + pr),
                dst_ref=cut_dst(me),
                send_sem=send_sem.at[n],
                recv_sem=recv_sem.at[n],
                device_id=(ps, pr),
                device_id_type=MESH,
            ).start()
            return carry

        lax.fori_loop(1, DEVS, send, 0)

    def wait_recv(ref, n):
        pltpu.make_async_copy(ref, ref, recv_sem.at[n]).wait()

    def wait_send(ref, n):
        pltpu.make_async_copy(ref, ref, send_sem.at[n]).wait()

    for ts in range(BANDS):
        x_copy(ts).wait()
        transform(ts)
        if ts == 0:
            pl.semaphore_wait(pltpu.get_barrier_semaphore(), DEVS - 1)
        send_all(
            lambda d, ts=ts: s1.at[d, ts, pl.ds(0, 2)],
            lambda d, ts=ts: r1.at[d, ts, pl.ds(0, 2)],
            ts,
        )
    send_all(lambda d: s1.at[d, :, 2], lambda d: r1.at[d, :, 2], 3)

    lane = lane_of(BAND)

    def matrix_rows(i, ts, h):
        return pl.ds(pl.multiple_of(i * 96 + h * HALF + ts * BAND, BAND), BAND)

    def assemble(f):
        def step(n, carry):
            i, ts = n // BANDS, n % BANDS
            for jh in range(2):
                near, far = [], []
                for jj in range(8):
                    src = i * RCVS + jh * 8 + jj
                    a, b = r1[src, ts, f], r1[src, ts, f + 1]
                    mixed = jnp.where(lane < 64, b, a)
                    near.append(a if f == 0 else mixed)
                    far.append(mixed if f == 0 else b)
                for gl in range(4):
                    g = 4 * f + gl
                    t = [
                        turned((near if gl < 2 else far)[jj], 48 * (jj - g)) for jj in range(8)
                    ]
                    out = (
                        jnp.where(lane < 48, t[0], jnp.where(lane < 96, t[1], t[2])),
                        jnp.where(
                            lane < 64,
                            jnp.where(lane < 16, t[2], t[3]),
                            jnp.where(lane < 112, t[4], t[5]),
                        ),
                        jnp.where(lane < 32, t[5], jnp.where(lane < 80, t[6], t[7])),
                    )
                    rows = matrix_rows(i, ts, gl % 2)
                    for k in range(TILES):
                        mbuf[gl // 2, rows, pl.ds((jh * TILES + k) * LANES, LANES)] = out[k]
            return carry

        lax.fori_loop(0, SHOTS * BANDS, step, 0)

    def average_and_weight(f):
        def block_row(bi, carry):
            here = pl.ds(pl.multiple_of(bi * LANES, LANES), LANES)
            for bj in range(STATIONS // LANES):
                there = pl.ds(bj * LANES, LANES)
                parts = []
                for c in range(2):
                    both = mbuf[c, here, there].astype(F32) + mbuf[c, there, here].T.astype(F32)
                    parts.append((0.5 * both).astype(BF16))
                abuf[pl.ds(pl.multiple_of(STATIONS + bi * LANES, LANES), LANES), there] = parts[0]
                abuf[here, there] = parts[1]
                ar, ai = parts[0].astype(F32), parts[1].astype(F32)
                wr = weight[0, f : f + 1, there]
                wi = weight[1, f : f + 1, there]
                lr, li = wr * ar - wi * ai, wr * ai + wi * ar
                lbuf[here, there] = (-li).astype(BF16)
                lbuf[here, pl.ds(STATIONS + bj * LANES, LANES)] = lr.astype(BF16)
                lbuf[here, pl.ds(2 * STATIONS + bj * LANES, LANES)] = li.astype(BF16)
            return carry

        lax.fori_loop(0, STATIONS // LANES, block_row, 0)

    def multiply():
        def columns(n, carry):
            cols = pl.ds(pl.multiple_of(n * 256, 256), 256)
            rhs = abuf[:, cols]
            for c in range(2):
                lhs = lbuf[:, c * STATIONS : c * STATIONS + 2 * STATIONS]
                pbuf[c, :, cols] = jnp.dot(lhs, rhs, preferred_element_type=F32).astype(BF16)
            return carry

        lax.fori_loop(0, STATIONS // 256, columns, 0)

    def scatter(f):
        def step(n, carry):
            i, ts = n // BANDS, n % BANDS
            for jh in range(2):
                cut = []
                for gl in range(4):
                    rows = matrix_rows(i, ts, gl % 2)
                    p = [
                        pbuf[gl // 2, rows, pl.ds((jh * TILES + k) * LANES, LANES)]
                        for k in range(TILES)
                    ]
                    p01 = jnp.where(lane < 64, p[1], p[0])
                    p12 = jnp.where(lane < 64, p[2], p[1])
                    held = (p[0], p[0], p01, p[1], p[1], p12, p[2], p[2])
                    cut.append([turned(held[jj], 48 * (4 * f + gl - jj)) for jj in range(8)])
                for jj in range(8):
                    dst = i * RCVS + jh * 8 + jj
                    t = [cut[gl][jj] for gl in range(4)]
                    if f == 0:
                        s2[dst, ts, 0] = jnp.where(
                            lane < 48, t[0], jnp.where(lane < 96, t[1], t[2])
                        )
                        s2[dst, ts, 1] = jnp.where(lane < 16, t[2], t[3])
                    else:
                        s2[dst, ts, 1] = jnp.where(
                            lane < 64, s2[dst, ts, 1], jnp.where(lane < 112, t[0], t[1])
                        )
                        s2[dst, ts, 2] = jnp.where(
                            lane < 32, t[1], jnp.where(lane < 80, t[2], t[3])
                        )
            return carry

        lax.fori_loop(0, SHOTS * BANDS, step, 0)

    for ts in range(BANDS):
        wait_recv(r1.at[:, ts, pl.ds(0, 2)], ts)
    assemble(0)
    average_and_weight(0)
    multiply()
    scatter(0)
    send_all(lambda d: s2.at[d, :, 0], lambda d: back.at[d, :, 0], 4)
    wait_recv(r1.at[:, :, 2], 3)
    assemble(1)
    average_and_weight(1)
    multiply()
    scatter(1)
    send_all(lambda d: s2.at[d, :, pl.ds(1, 2)], lambda d: back.at[d, :, pl.ds(1, 2)], 5)

    others = pl.ds(0, DEVS - 1)
    for ts in range(BANDS):
        wait_send(s1.at[others, ts, pl.ds(0, 2)], ts)
    wait_send(s1.at[others, :, 2], 3)
    wait_send(s2.at[others, :, 0], 4)
    wait_send(s2.at[others, :, pl.ds(1, 2)], 5)
    wait_recv(back.at[:, :, 0], 4)
    wait_recv(back.at[:, :, pl.ds(1, 2)], 5)


def series_kernel(block, basis, out, wide, turn):
    def widen(g, carry):
        rows = block[pl.ds(g * 8, 8), 0].astype(F32).reshape(8 * ROWS_MSG, LANES)
        wide[pl.ds(pl.multiple_of(g * 8 * ROWS_MSG, 8 * ROWS_MSG), 8 * ROWS_MSG), :] = rows
        return carry

    lax.fori_loop(0, DEVS // 8, widen, 0)

    def swap(s, carry):
        tiles = [
            wide[pl.ds(k * BAND + s, DEVS, stride=ROWS_MSG), :].T for k in range(TILES)
        ]
        flat = jnp.concatenate(tiles, 0).astype(BF16)
        rows = pl.ds(pl.multiple_of(s * 96, 96), 96)
        for q in range(4):
            turn[rows, q * DEVS : (q + 1) * DEVS] = flat[96 * q : 96 * (q + 1)]
        return carry

    lax.fori_loop(0, BAND, swap, 0)

    def series(m, carry):
        rows = pl.ds(pl.multiple_of(m * 384, 384), 384)
        value = jnp.dot(turn[rows, :], basis[...], preferred_element_type=F32)
        value = (value * (2.0 / SAMPLES) ** 0.5).astype(BF16)
        for s in range(4):
            for h in range(2):
                low = s * 96 + h * HALF
                out[h, m * 4 + s] = value[low : low + HALF]
        return carry

    lax.fori_loop(0, BAND // 4, series, 0)


def on_device(traces, source_weight):
    basis = basis_table()
    halves = traces.reshape(2, HALF, HALF, SAMPLES)
    back = pl.pallas_call(
        predict_kernel,
        name="predict",
        out_shape=jax.ShapeDtypeStruct((DEVS, BANDS, TILES, BAND, LANES), BF16),
        in_specs=[
            pl.BlockSpec(memory_space=pl.ANY),
            pl.BlockSpec(memory_space=pltpu.VMEM),
            pl.BlockSpec(memory_space=pltpu.VMEM),
        ],
        out_specs=pl.BlockSpec(memory_space=pl.ANY),
        scratch_shapes=[
            pltpu.VMEM((2, HALF, HALF, SAMPLES), BF16),
            pltpu.VMEM((DEVS * ROWS_MSG, LANES), F32),
            pltpu.VMEM((DEVS, BANDS, TILES, BAND, LANES), BF16),
            pltpu.VMEM((DEVS, BANDS, TILES, BAND, LANES), BF16),
            pltpu.VMEM((2, STATIONS, STATIONS), BF16),
            pltpu.VMEM((2 * STATIONS, STATIONS), BF16),
            pltpu.VMEM((STATIONS, 3 * STATIONS), BF16),
            pltpu.VMEM((2, STATIONS, STATIONS), BF16),
            pltpu.VMEM((DEVS, BANDS, TILES, BAND, LANES), BF16),
            pltpu.SemaphoreType.DMA((BANDS,)),
            pltpu.SemaphoreType.DMA((6,)),
            pltpu.SemaphoreType.DMA((6,)),
        ],
        compiler_params=pltpu.CompilerParams(
            collective_id=0, has_side_effects=True, vmem_limit_bytes=56 * 1024 * 1024
        ),
    )(halves, basis, source_weight)
    series = pl.pallas_call(
        series_kernel,
        name="series",
        grid=(BANDS,),
        out_shape=jax.ShapeDtypeStruct((2, HALF, HALF, SAMPLES), BF16),
        in_specs=[
            pl.BlockSpec((DEVS, 1, TILES, BAND, LANES), lambda b: (0, b, 0, 0, 0)),
            pl.BlockSpec((2 * FREQS, SAMPLES), lambda b: (0, 0)),
        ],
        out_specs=pl.BlockSpec((2, BAND, HALF, SAMPLES), lambda b: (0, b, 0, 0)),
        scratch_shapes=[
            pltpu.VMEM((DEVS * ROWS_MSG, LANES), F32),
            pltpu.VMEM((BAND * 96, 2 * FREQS), BF16),
        ],
        compiler_params=pltpu.CompilerParams(vmem_limit_bytes=40 * 1024 * 1024),
    )(back, basis)
    return series.reshape(2 * HALF, HALF, SAMPLES)


def solution(mesh):
    placed = (P("shot", "rcv", None), P(None, ("shot", "rcv"), None))
    return jax.shard_map(
        on_device, mesh=mesh, in_specs=placed, out_specs=P("shot", "rcv", None), check_vma=False
    )
```

time: 347 us -> 153 us (0.44)
  Pallas kernels: 0 us -> 149 us
  local copies, waits for them, and re-layouts: 132 us -> 2.33 us
  blocking collectives: 80.6 us -> 0 us
  waiting for transfers between devices: 75.8 us -> 0 us
  matrix products: 24.1 us -> 0 us
  other arithmetic: 20 us -> 0 us
  starting transfers between devices: 10.9 us -> 0 us
    pallas_call x0 -> x2, Pallas kernels: none -> 149 us  [the longest x1 134 us: on_device(): pl.pallas_call(predict_kernel, name='predict', out_shape=jax.ShapeDtypeSt...]
    all_to_all x1 -> x0, blocking collectives: 80.6 us -> none  [on_device(): lax.all_to_all(outgoing, ('shot', 'rcv'), split_axis=3, concat_axis=0, ti...]
    all_to_all x1 -> x0, waiting for transfers between devices: 75.8 us -> none  [on_device(): lax.all_to_all(spectra, ('shot', 'rcv'), split_axis=0, concat_axis=3, til...]
    reshape x5 -> x0, local copies, waits for them, and re-layouts: 72.5 us -> none  [the longest x2 30.1 us: on_device(): spectra = (spectra * samples ** (-0.5)).astype(jnp.bfloat16).reshape(freq...]
    dot_general x4 -> x0, matrix products: 24.1 us -> none  [the longest x2 10.6 us: predict_single(): jnp.dot(left_operand, second_factor, preferred_element_type=jnp.float32)]
    all_to_all x3 -> x0, local copies, waits for them, and re-layouts: 22.7 us -> none  [the longest x2 16.2 us: on_device(): lax.all_to_all(outgoing, ('shot', 'rcv'), split_axis=3, concat_axis=0, ti...]
    convert_element_type x5 -> x0, local copies, waits for them, and re-layouts: 22.2 us -> none  [the longest x2 12.1 us: predict_single(): one_slice.astype(jnp.float32)]
    convert_element_type x6 -> x0, other arithmetic: 16.6 us -> none  [the longest x2 8.38 us: predict_single(): one_slice.astype(jnp.float32)]
  transfers between devices with their start and end apart: 1 -> 0, of which waited for: 1 -> 0; matrix products, arithmetic and copies ran while one was open for 0% -> 0% of each run, Pallas kernels for 0% -> 0%
where the time goes in v1:
time: 153 us; the launch traced here: 151 us
  Pallas kernels  149 us (97%)
  local copies, waits for them, and re-layouts  2.33 us (2%)
    pallas_call x1, Pallas kernels, on_device(): pl.pallas_call(predict_kernel, name='predict', out_shape=jax.ShapeDtypeSt...  134 us
    pallas_call x1, Pallas kernels, on_device(): pl.pallas_call(series_kernel, name='series', grid=(BANDS,), out_shape=jax...  15 us

profile of v1, /device:TPU:2, one launch (start us, length us, event | category | flops | bytes accessed | tf_op | source)
XLA Modules:
  0.0 151.2 jit_solution(14973579583543375067)
XLA Ops:
  0.0 0.0 copy-start.1
  0.0 133.8 %predict.1.block = bf16[128,3,3,16,128]{4,3,2,1,0:T(8,128)(2,1)} custom-call(bf16[2,48,48,512]{3,2,1,0:T(8,128)(2,1)} %bitcast.2, bf16[512,512]{1,0:T(8,128)(2,1)} %constant.2.clone.basis, f32[2,2,768]{2,1,0:T(2,128)} %weight.1), custom_call_target="tpu_custom_call" | custom-call | tf_op jit(solution)/shard_map/predict/pallas_call | solution.py:313
  133.8 0.0 copy-done.1
  133.8 0.0 copy-start
  133.9 2.3 %copy-done = bf16[128,3,3,16,128]{4,3,2,1,0:T(8,128)(2,1)S(1)} copy-done((bf16[128,3,3,16,128]{4,3,2,1,0:T(8,128)(2,1)S(1)}, bf16[128,3,3,16,128]{4,3,2,1,0:T(8,128)(2,1)}, u32[]{:S(2)}) %copy-start) | copy-done | bytes 4718616
  136.2 15.0 %series.1 = bf16[2,48,48,512]{3,2,1,0:T(8,128)(2,1)} custom-call(bf16[128,3,3,16,128]{4,3,2,1,0:T(8,128)(2,1)S(1)} %copy-done, bf16[512,512]{1,0:T(8,128)(2,1)S(1)} %copy-done.1), custom_call_target="tpu_custom_call" | custom-call | tf_op jit(solution)/shard_map/series/pallas_call | solution.py:341
Async XLA Ops:
  0.0 133.8 %copy-start.1 = (bf16[512,512]{1,0:T(8,128)(2,1)S(1)}, bf16[512,512]{1,0:T(8,128)(2,1)}, u32[]{:S(2)}) copy-start(bf16[512,512]{1,0:T(8,128)(2,1)} %constant.2.clone.basis) | copy-start | bytes 1572868
  133.8 2.3 %copy-start = (bf16[128,3,3,16,128]{4,3,2,1,0:T(8,128)(2,1)S(1)}, bf16[128,3,3,16,128]{4,3,2,1,0:T(8,128)(2,1)}, u32[]{:S(2)}) copy-start(bf16[128,3,3,16,128]{4,3,2,1,0:T(8,128)(2,1)} %predict.1.block) | copy-start | bytes 14155780

commit v2 on v1

--- a/solution.py
+++ b/solution.py
@@ -44,38 +44,41 @@
     return tile if amount == 0 else pltpu.roll(tile, amount, 1)
 
 
-def peer(step):
-    v = (step * 63) % DEVS
-    bits = [(v // (1 << b)) % 2 for b in range(7)]
-    dx, dy, dz, dc = 2 * bits[0] + bits[5], 2 * bits[1] + bits[2], 2 * bits[6] + bits[4], bits[3]
+def peers_in_order():
     shot, rcv = lax.axis_index("shot"), lax.axis_index("rcv")
-    x = ((rcv // 2) % 4 + dx) % 4
-    y = ((rcv // 8) * 2 + shot % 2 + dy) % 4
-    z = (shot // 2 + dz) % 4
-    c = (rcv % 2 + dc) % 2
-    return z * 2 + y % 2, (y // 2) * 8 + x * 2 + c
+    x, y, z, c = (rcv // 2) % 4, (rcv // 8) * 2 + shot % 2, shot // 2, rcv % 2
+    xs = [2 * ((x + d) % 4) for d in range(4)]
+    ys = [((y + d) % 4 % 2, (y + d) % 4 // 2 * 8) for d in range(4)]
+    zs = [2 * ((z + d) % 4) for d in range(4)]
+    cs = [(c + d) % 2 for d in range(2)]
+    order = []
+    for step in range(1, DEVS):
+        v = step * 63 % DEVS
+        bit = [(v >> b) & 1 for b in range(7)]
+        dx, dy, dz = 2 * bit[0] + bit[5], 2 * bit[1] + bit[2], 2 * bit[6] + bit[4]
+        order.append((zs[dz] + ys[dy][0], ys[dy][1] + xs[dx] + cs[bit[3]]))
+    return order
 
 
 def predict_kernel(
     x_hbm, basis, weight, back, xbuf, fbuf, s1, r1, mbuf, abuf, lbuf, pbuf, s2,
-    xsem, send_sem, recv_sem,
+    table, xsem, send_sem, recv_sem,
 ):
     shot, rcv = lax.axis_index("shot"), lax.axis_index("rcv")
     me = shot * RCVS + rcv
 
-    def greet(step, carry):
-        pl.semaphore_signal(
-            pltpu.get_barrier_semaphore(), inc=1, device_id=peer(step), device_id_type=MESH
-        )
-        return carry
-
     def x_copy(ts):
         band = pl.ds(ts * BAND, BAND)
         return pltpu.make_async_copy(x_hbm.at[:, band], xbuf.at[:, band], xsem.at[ts])
 
     for ts in range(BANDS):
         x_copy(ts).start()
-    lax.fori_loop(1, DEVS, greet, 0)
+    for step, (ps, pr) in enumerate(peers_in_order()):
+        pl.semaphore_signal(
+            pltpu.get_barrier_semaphore(), inc=1, device_id=(ps, pr), device_id_type=MESH
+        )
+        table[2 * step] = ps
+        table[2 * step + 1] = pr
 
     def transform(ts):
         def pair(u, carry):
@@ -101,7 +104,7 @@
                     )
             return carry
 
-        lax.fori_loop(0, BAND // 2, pair, 0)
+        lax.fori_loop(0, BAND // 2, pair, 0, unroll=8)
 
         def narrow(g, carry):
             rows = fbuf[pl.ds(pl.multiple_of(g * 8 * ROWS_MSG, 8 * ROWS_MSG), 8 * ROWS_MSG), :]
@@ -115,7 +118,7 @@
         local.start()
 
         def send(step, carry):
-            ps, pr = peer(step)
+            ps, pr = table[2 * step], table[2 * step + 1]
             pltpu.make_async_remote_copy(
                 src_ref=cut_src(ps * RCVS + pr),
                 dst_ref=cut_dst(me),
@@ -126,7 +129,7 @@
             ).start()
             return carry
 
-        lax.fori_loop(1, DEVS, send, 0)
+        lax.fori_loop(0, DEVS - 1, send, 0)
 
     def wait_recv(ref, n):
         pltpu.make_async_copy(ref, ref, recv_sem.at[n]).wait()
@@ -284,15 +287,15 @@
 
     def swap(s, carry):
         tiles = [
-            wide[pl.ds(k * BAND + s, DEVS, stride=ROWS_MSG), :].T for k in range(TILES)
+            wide[pl.ds(k * BAND + s, DEVS, stride=ROWS_MSG), :].astype(BF16).T for k in range(TILES)
         ]
-        flat = jnp.concatenate(tiles, 0).astype(BF16)
+        flat = jnp.concatenate(tiles, 0)
         rows = pl.ds(pl.multiple_of(s * 96, 96), 96)
         for q in range(4):
             turn[rows, q * DEVS : (q + 1) * DEVS] = flat[96 * q : 96 * (q + 1)]
         return carry
 
-    lax.fori_loop(0, BAND, swap, 0)
+    lax.fori_loop(0, BAND, swap, 0, unroll=16)
 
     def series(m, carry):
         rows = pl.ds(pl.multiple_of(m * 384, 384), 384)
@@ -304,7 +307,7 @@
                 out[h, m * 4 + s] = value[low : low + HALF]
         return carry
 
-    lax.fori_loop(0, BAND // 4, series, 0)
+    lax.fori_loop(0, BAND // 4, series, 0, unroll=2)
 
 
 def on_device(traces, source_weight):
@@ -330,6 +333,7 @@
             pltpu.VMEM((STATIONS, 3 * STATIONS), BF16),
             pltpu.VMEM((2, STATIONS, STATIONS), BF16),
             pltpu.VMEM((DEVS, BANDS, TILES, BAND, LANES), BF16),
+            pltpu.SMEM((2 * DEVS,), jnp.int32),
             pltpu.SemaphoreType.DMA((BANDS,)),
             pltpu.SemaphoreType.DMA((6,)),
             pltpu.SemaphoreType.DMA((6,)),

time: 153 us -> 142 us (0.928); the launches traced: 151 us -> 142 us
  Pallas kernels: 149 us -> 140 us
    pallas_call x1, Pallas kernels: 15 us -> 9.62 us  [on_device(): pl.pallas_call(series_kernel, name='series', grid=(BANDS,), out_shape=jax...]
    pallas_call x1, Pallas kernels: 134 us -> 130 us  [on_device(): pl.pallas_call(predict_kernel, name='predict', out_shape=jax.ShapeDtypeSt...]
where the time goes in v2:
time: 142 us
  Pallas kernels  140 us (99%)
  local copies, waits for them, and re-layouts  2.33 us (2%)
    pallas_call x1, Pallas kernels, on_device(): pl.pallas_call(predict_kernel, name='predict', out_shape=jax.ShapeDtypeSt...  130 us
    pallas_call x1, Pallas kernels, on_device(): pl.pallas_call(series_kernel, name='series', grid=(BANDS,), out_shape=jax...  9.62 us

profile of v2, /device:TPU:2, one launch (start us, length us, event | category | flops | bytes accessed | tf_op | source)
XLA Modules:
  0.0 142.2 jit_solution(2683050100548744880)
XLA Ops:
  0.0 0.0 copy-start.1
  0.0 130.2 %predict.1.block = bf16[128,3,3,16,128]{4,3,2,1,0:T(8,128)(2,1)} custom-call(bf16[2,48,48,512]{3,2,1,0:T(8,128)(2,1)} %bitcast.2, bf16[512,512]{1,0:T(8,128)(2,1)} %constant.2.clone.basis, f32[2,2,768]{2,1,0:T(2,128)} %weight.1), custom_call_target="tpu_custom_call" | custom-call | tf_op jit(solution)/shard_map/predict/pallas_call | solution.py:316
  130.2 0.0 copy-done.1
  130.2 0.0 copy-start
  130.2 2.3 %copy-done = bf16[128,3,3,16,128]{4,3,2,1,0:T(8,128)(2,1)S(1)} copy-done((bf16[128,3,3,16,128]{4,3,2,1,0:T(8,128)(2,1)S(1)}, bf16[128,3,3,16,128]{4,3,2,1,0:T(8,128)(2,1)}, u32[]{:S(2)}) %copy-start) | copy-done | bytes 4718616
  132.6 9.6 %series.1 = bf16[2,48,48,512]{3,2,1,0:T(8,128)(2,1)} custom-call(bf16[128,3,3,16,128]{4,3,2,1,0:T(8,128)(2,1)S(1)} %copy-done, bf16[512,512]{1,0:T(8,128)(2,1)S(1)} %copy-done.1), custom_call_target="tpu_custom_call" | custom-call | tf_op jit(solution)/shard_map/series/pallas_call | solution.py:345
Async XLA Ops:
  0.0 130.2 %copy-start.1 = (bf16[512,512]{1,0:T(8,128)(2,1)S(1)}, bf16[512,512]{1,0:T(8,128)(2,1)}, u32[]{:S(2)}) copy-start(bf16[512,512]{1,0:T(8,128)(2,1)} %constant.2.clone.basis) | copy-start | bytes 1572868
  130.2 2.3 %copy-start = (bf16[128,3,3,16,128]{4,3,2,1,0:T(8,128)(2,1)S(1)}, bf16[128,3,3,16,128]{4,3,2,1,0:T(8,128)(2,1)}, u32[]{:S(2)}) copy-start(bf16[128,3,3,16,128]{4,3,2,1,0:T(8,128)(2,1)} %predict.1.block) | copy-start | bytes 14155780

commit v3 on v2

--- a/solution.py
+++ b/solution.py
@@ -61,8 +61,8 @@
 
 
 def predict_kernel(
-    x_hbm, basis, weight, back, xbuf, fbuf, s1, r1, mbuf, abuf, lbuf, pbuf, s2,
-    table, xsem, send_sem, recv_sem,
+    x_hbm, basis, weight, out_hbm, xbuf, fbuf, s1, r1, mbuf, abuf, lbuf, pbuf, s2, back,
+    turn, obuf, table, xsem, osem, send_sem, recv_sem,
 ):
     shot, rcv = lax.axis_index("shot"), lax.axis_index("rcv")
     me = shot * RCVS + rcv
@@ -113,15 +113,16 @@
 
         lax.fori_loop(0, DEVS // 8, narrow, 0)
 
-    def send_all(cut_src, cut_dst, n):
-        local = pltpu.make_async_copy(cut_src(me), cut_dst(me), recv_sem.at[n])
-        local.start()
+    def send_all(src, dst, n, bands, tiles):
+        pltpu.make_async_copy(
+            src.at[me, bands, tiles], dst.at[me, bands, tiles], recv_sem.at[n]
+        ).start()
 
         def send(step, carry):
             ps, pr = table[2 * step], table[2 * step + 1]
             pltpu.make_async_remote_copy(
-                src_ref=cut_src(ps * RCVS + pr),
-                dst_ref=cut_dst(me),
+                src_ref=src.at[ps * RCVS + pr, bands, tiles],
+                dst_ref=dst.at[me, bands, tiles],
                 send_sem=send_sem.at[n],
                 recv_sem=recv_sem.at[n],
                 device_id=(ps, pr),
@@ -131,23 +132,24 @@
 
         lax.fori_loop(0, DEVS - 1, send, 0)
 
-    def wait_recv(ref, n):
+    def wait_recv(dst, n, bands, tiles):
+        ref = dst.at[:, bands, tiles]
         pltpu.make_async_copy(ref, ref, recv_sem.at[n]).wait()
 
-    def wait_send(ref, n):
+    def wait_send(src, n, bands, tiles):
+        ref = src.at[pl.ds(0, DEVS - 1), bands, tiles]
         pltpu.make_async_copy(ref, ref, send_sem.at[n]).wait()
 
-    for ts in range(BANDS):
+    first, later, lead = pl.ds(0, 1), pl.ds(1, BANDS - 1), pl.ds(0, BANDS - 1)
+    x_copy(0).wait()
+    transform(0)
+    pl.semaphore_wait(pltpu.get_barrier_semaphore(), DEVS - 1)
+    send_all(s1, r1, 0, first, pl.ds(0, 2))
+    for ts in range(1, BANDS):
         x_copy(ts).wait()
         transform(ts)
-        if ts == 0:
-            pl.semaphore_wait(pltpu.get_barrier_semaphore(), DEVS - 1)
-        send_all(
-            lambda d, ts=ts: s1.at[d, ts, pl.ds(0, 2)],
-            lambda d, ts=ts: r1.at[d, ts, pl.ds(0, 2)],
-            ts,
-        )
-    send_all(lambda d: s1.at[d, :, 2], lambda d: r1.at[d, :, 2], 3)
+    send_all(s1, r1, 1, later, pl.ds(0, 2))
+    send_all(s1, r1, 2, pl.ds(0, BANDS), pl.ds(2, 1))
 
     lane = lane_of(BAND)
 
@@ -253,70 +255,79 @@
 
         lax.fori_loop(0, SHOTS * BANDS, step, 0)
 
-    for ts in range(BANDS):
-        wait_recv(r1.at[:, ts, pl.ds(0, 2)], ts)
+    def series(ts):
+        flat_back = back.reshape(DEVS * BANDS * ROWS_MSG, LANES)
+
+        def swap(row, carry):
+            tiles = [
+                flat_back[
+                    pl.ds((ts * TILES + k) * BAND + row, DEVS, stride=BANDS * ROWS_MSG), :
+                ].T
+                for k in range(TILES)
+            ]
+            flat = jnp.concatenate(tiles, 0)
+            rows = pl.ds(pl.multiple_of(row * 96, 96), 96)
+            for q in range(4):
+                turn[rows, q * DEVS : (q + 1) * DEVS] = flat[96 * q : 96 * (q + 1)]
+            return carry
+
+        lax.fori_loop(0, BAND, swap, 0, unroll=16)
+
+        def values(m, carry):
+            rows = pl.ds(pl.multiple_of(m * 384, 384), 384)
+            value = jnp.dot(turn[rows, :], basis[...], preferred_element_type=F32)
+            value = (value * (2.0 / SAMPLES) ** 0.5).astype(BF16)
+            for s in range(4):
+                for h in range(2):
+                    low = s * 96 + h * HALF
+                    obuf[h, ts * BAND + m * 4 + s] = value[low : low + HALF]
+            return carry
+
+        lax.fori_loop(0, BAND // 4, values, 0, unroll=2)
+        out_copy(ts).start()
+
+    def out_copy(ts):
+        band = pl.ds(ts * BAND, BAND)
+        return pltpu.make_async_copy(obuf.at[:, band], out_hbm.at[:, band], osem.at[ts])
+
+    everything = pl.ds(0, BANDS)
+    wait_recv(r1, 0, first, pl.ds(0, 2))
+    wait_recv(r1, 1, later, pl.ds(0, 2))
     assemble(0)
     average_and_weight(0)
     multiply()
     scatter(0)
-    send_all(lambda d: s2.at[d, :, 0], lambda d: back.at[d, :, 0], 4)
-    wait_recv(r1.at[:, :, 2], 3)
+    send_all(s2, back, 3, everything, pl.ds(0, 1))
+    wait_recv(r1, 2, everything, pl.ds(2, 1))
     assemble(1)
     average_and_weight(1)
     multiply()
     scatter(1)
-    send_all(lambda d: s2.at[d, :, pl.ds(1, 2)], lambda d: back.at[d, :, pl.ds(1, 2)], 5)
-
-    others = pl.ds(0, DEVS - 1)
+    send_all(s2, back, 4, lead, pl.ds(1, 2))
+    send_all(s2, back, 5, pl.ds(BANDS - 1, 1), pl.ds(1, 2))
+    wait_send(s1, 0, first, pl.ds(0, 2))
+    wait_send(s1, 1, later, pl.ds(0, 2))
+    wait_send(s1, 2, everything, pl.ds(2, 1))
+    wait_send(s2, 3, everything, pl.ds(0, 1))
+    wait_recv(back, 3, everything, pl.ds(0, 1))
+    wait_recv(back, 4, lead, pl.ds(1, 2))
+    for ts in range(BANDS - 1):
+        series(ts)
+    wait_send(s2, 4, lead, pl.ds(1, 2))
+    wait_recv(back, 5, pl.ds(BANDS - 1, 1), pl.ds(1, 2))
+    series(BANDS - 1)
+    wait_send(s2, 5, pl.ds(BANDS - 1, 1), pl.ds(1, 2))
     for ts in range(BANDS):
-        wait_send(s1.at[others, ts, pl.ds(0, 2)], ts)
-    wait_send(s1.at[others, :, 2], 3)
-    wait_send(s2.at[others, :, 0], 4)
-    wait_send(s2.at[others, :, pl.ds(1, 2)], 5)
-    wait_recv(back.at[:, :, 0], 4)
-    wait_recv(back.at[:, :, pl.ds(1, 2)], 5)
-
-
-def series_kernel(block, basis, out, wide, turn):
-    def widen(g, carry):
-        rows = block[pl.ds(g * 8, 8), 0].astype(F32).reshape(8 * ROWS_MSG, LANES)
-        wide[pl.ds(pl.multiple_of(g * 8 * ROWS_MSG, 8 * ROWS_MSG), 8 * ROWS_MSG), :] = rows
-        return carry
-
-    lax.fori_loop(0, DEVS // 8, widen, 0)
-
-    def swap(s, carry):
-        tiles = [
-            wide[pl.ds(k * BAND + s, DEVS, stride=ROWS_MSG), :].astype(BF16).T for k in range(TILES)
-        ]
-        flat = jnp.concatenate(tiles, 0)
-        rows = pl.ds(pl.multiple_of(s * 96, 96), 96)
-        for q in range(4):
-            turn[rows, q * DEVS : (q + 1) * DEVS] = flat[96 * q : 96 * (q + 1)]
-        return carry
-
-    lax.fori_loop(0, BAND, swap, 0, unroll=16)
-
-    def series(m, carry):
-        rows = pl.ds(pl.multiple_of(m * 384, 384), 384)
-        value = jnp.dot(turn[rows, :], basis[...], preferred_element_type=F32)
-        value = (value * (2.0 / SAMPLES) ** 0.5).astype(BF16)
-        for s in range(4):
-            for h in range(2):
-                low = s * 96 + h * HALF
-                out[h, m * 4 + s] = value[low : low + HALF]
-        return carry
-
-    lax.fori_loop(0, BAND // 4, series, 0, unroll=2)
+        out_copy(ts).wait()
 
 
 def on_device(traces, source_weight):
     basis = basis_table()
     halves = traces.reshape(2, HALF, HALF, SAMPLES)
-    back = pl.pallas_call(
+    series = pl.pallas_call(
         predict_kernel,
         name="predict",
-        out_shape=jax.ShapeDtypeStruct((DEVS, BANDS, TILES, BAND, LANES), BF16),
+        out_shape=jax.ShapeDtypeStruct((2, HALF, HALF, SAMPLES), BF16),
         in_specs=[
             pl.BlockSpec(memory_space=pl.ANY),
             pl.BlockSpec(memory_space=pltpu.VMEM),
@@ -333,7 +344,11 @@
             pltpu.VMEM((STATIONS, 3 * STATIONS), BF16),
             pltpu.VMEM((2, STATIONS, STATIONS), BF16),
             pltpu.VMEM((DEVS, BANDS, TILES, BAND, LANES), BF16),
+            pltpu.VMEM((DEVS, BANDS, TILES, BAND, LANES), BF16),
+            pltpu.VMEM((BAND * 96, 2 * FREQS), BF16),
+            pltpu.VMEM((2, HALF, HALF, SAMPLES), BF16),
             pltpu.SMEM((2 * DEVS,), jnp.int32),
+            pltpu.SemaphoreType.DMA((BANDS,)),
             pltpu.SemaphoreType.DMA((BANDS,)),
             pltpu.SemaphoreType.DMA((6,)),
             pltpu.SemaphoreType.DMA((6,)),
@@ -342,22 +357,6 @@
             collective_id=0, has_side_effects=True, vmem_limit_bytes=56 * 1024 * 1024
         ),
     )(halves, basis, source_weight)
-    series = pl.pallas_call(
-        series_kernel,
-        name="series",
-        grid=(BANDS,),
-        out_shape=jax.ShapeDtypeStruct((2, HALF, HALF, SAMPLES), BF16),
-        in_specs=[
-            pl.BlockSpec((DEVS, 1, TILES, BAND, LANES), lambda b: (0, b, 0, 0, 0)),
-            pl.BlockSpec((2 * FREQS, SAMPLES), lambda b: (0, 0)),
-        ],
-        out_specs=pl.BlockSpec((2, BAND, HALF, SAMPLES), lambda b: (0, b, 0, 0)),
-        scratch_shapes=[
-            pltpu.VMEM((DEVS * ROWS_MSG, LANES), F32),
-            pltpu.VMEM((BAND * 96, 2 * FREQS), BF16),
-        ],
-        compiler_params=pltpu.CompilerParams(vmem_limit_bytes=40 * 1024 * 1024),
-    )(back, basis)
     return series.reshape(2 * HALF, HALF, SAMPLES)
 
 

time: 142 us -> 129 us (0.908)
  Pallas kernels: 140 us -> 124 us
  local copies, waits for them, and re-layouts: 2.33 us -> 4.85 us
    pallas_call x1 -> x0, Pallas kernels: 9.62 us -> none  [on_device(): pl.pallas_call(series_kernel, name='series', grid=(BANDS,), out_shape=jax...]
    pallas_call x1, Pallas kernels: 130 us -> 124 us  [on_device(): pl.pallas_call(predict_kernel, name='predict', out_shape=jax.ShapeDtypeSt...]
    unnamed x4 -> x1, local copies, waits for them, and re-layouts: 2.33 us -> 4.85 us
where the time goes in v3:
time: 129 us
  Pallas kernels  124 us (96%)
  local copies, waits for them, and re-layouts  4.85 us (4%)
    pallas_call x1, Pallas kernels, on_device(): pl.pallas_call(predict_kernel, name='predict', out_shape=jax.ShapeDtypeSt...  124 us
    unnamed x1, local copies, waits for them, and re-layouts  4.85 us

profile of v3, /device:TPU:2, one launch (start us, length us, event | category | flops | bytes accessed | tf_op | source)
XLA Modules:
  0.0 128.9 jit_solution(5973192334791249736)
XLA Ops:
  0.0 124.1 %predict.1 = bf16[2,48,48,512]{3,2,1,0:T(8,128)(2,1)} custom-call(bf16[2,48,48,512]{3,2,1,0:T(8,128)(2,1)} %bitcast.3, bf16[512,512]{1,0:T(8,128)(2,1)} %constant.2.clone.basis, f32[2,2,768]{2,1,0:T(2,128)} %weight.1), custom_call_target="tpu_custom_call" | custom-call | tf_op jit(solution)/shard_map/predict/pallas_call | solution.py:327
  124.1 4.8 %copy.5 = bf16[96,48,512]{2,1,0:T(8,128)(2,1)} copy(bf16[96,48,512]{2,1,0:T(8,128)(2,1)} %bitcast.2) | data formatting | bytes 9437184

commit v4 on v3

--- a/solution.py
+++ b/solution.py
@@ -61,8 +61,8 @@
 
 
 def predict_kernel(
-    x_hbm, basis, weight, out_hbm, xbuf, fbuf, s1, r1, mbuf, abuf, lbuf, pbuf, s2, back,
-    turn, obuf, table, xsem, osem, send_sem, recv_sem,
+    x_hbm, basis_hbm, weight_hbm, obuf, basis, weight, xbuf, fbuf, s1, r1, mbuf, abuf, lbuf, pbuf, s2, back,
+    turn, table, xsem, psem, send_sem, recv_sem,
 ):
     shot, rcv = lax.axis_index("shot"), lax.axis_index("rcv")
     me = shot * RCVS + rcv
@@ -71,8 +71,13 @@
         band = pl.ds(ts * BAND, BAND)
         return pltpu.make_async_copy(x_hbm.at[:, band], xbuf.at[:, band], xsem.at[ts])
 
-    for ts in range(BANDS):
+    basis_copy = pltpu.make_async_copy(basis_hbm, basis, psem.at[0])
+    weight_copy = pltpu.make_async_copy(weight_hbm, weight, psem.at[1])
+    x_copy(0).start()
+    basis_copy.start()
+    for ts in range(1, BANDS):
         x_copy(ts).start()
+    weight_copy.start()
     for step, (ps, pr) in enumerate(peers_in_order()):
         pl.semaphore_signal(
             pltpu.get_barrier_semaphore(), inc=1, device_id=(ps, pr), device_id_type=MESH
@@ -141,6 +146,7 @@
         pltpu.make_async_copy(ref, ref, send_sem.at[n]).wait()
 
     first, later, lead = pl.ds(0, 1), pl.ds(1, BANDS - 1), pl.ds(0, BANDS - 1)
+    basis_copy.wait()
     x_copy(0).wait()
     transform(0)
     pl.semaphore_wait(pltpu.get_barrier_semaphore(), DEVS - 1)
@@ -258,39 +264,30 @@
     def series(ts):
         flat_back = back.reshape(DEVS * BANDS * ROWS_MSG, LANES)
 
-        def swap(row, carry):
-            tiles = [
-                flat_back[
-                    pl.ds((ts * TILES + k) * BAND + row, DEVS, stride=BANDS * ROWS_MSG), :
-                ].T
-                for k in range(TILES)
-            ]
-            flat = jnp.concatenate(tiles, 0)
-            rows = pl.ds(pl.multiple_of(row * 96, 96), 96)
-            for q in range(4):
-                turn[rows, q * DEVS : (q + 1) * DEVS] = flat[96 * q : 96 * (q + 1)]
-            return carry
-
-        lax.fori_loop(0, BAND, swap, 0, unroll=16)
-
-        def values(m, carry):
-            rows = pl.ds(pl.multiple_of(m * 384, 384), 384)
-            value = jnp.dot(turn[rows, :], basis[...], preferred_element_type=F32)
+        for m in range(BAND // 4):
+            for row in range(4 * m, 4 * m + 4):
+                tiles = [
+                    flat_back[
+                        pl.ds((ts * TILES + k) * BAND + row, DEVS, stride=BANDS * ROWS_MSG), :
+                    ].T
+                    for k in range(TILES)
+                ]
+                flat = jnp.concatenate(tiles, 0)
+                for q in range(4):
+                    turn[row * 96 : (row + 1) * 96, q * DEVS : (q + 1) * DEVS] = flat[
+                        96 * q : 96 * (q + 1)
+                    ]
+            value = jnp.dot(
+                turn[m * 384 : (m + 1) * 384, :], basis[...], preferred_element_type=F32
+            )
             value = (value * (2.0 / SAMPLES) ** 0.5).astype(BF16)
             for s in range(4):
                 for h in range(2):
                     low = s * 96 + h * HALF
                     obuf[h, ts * BAND + m * 4 + s] = value[low : low + HALF]
-            return carry
-
-        lax.fori_loop(0, BAND // 4, values, 0, unroll=2)
-        out_copy(ts).start()
-
-    def out_copy(ts):
-        band = pl.ds(ts * BAND, BAND)
-        return pltpu.make_async_copy(obuf.at[:, band], out_hbm.at[:, band], osem.at[ts])
 
     everything = pl.ds(0, BANDS)
+    weight_copy.wait()
     wait_recv(r1, 0, first, pl.ds(0, 2))
     wait_recv(r1, 1, later, pl.ds(0, 2))
     assemble(0)
@@ -317,8 +314,10 @@
     wait_recv(back, 5, pl.ds(BANDS - 1, 1), pl.ds(1, 2))
     series(BANDS - 1)
     wait_send(s2, 5, pl.ds(BANDS - 1, 1), pl.ds(1, 2))
-    for ts in range(BANDS):
-        out_copy(ts).wait()
+
+
+def in_hbm(array):
+    return pltpu.with_memory_space_constraint(array, pltpu.HBM)
 
 
 def on_device(traces, source_weight):
@@ -328,13 +327,11 @@
         predict_kernel,
         name="predict",
         out_shape=jax.ShapeDtypeStruct((2, HALF, HALF, SAMPLES), BF16),
-        in_specs=[
-            pl.BlockSpec(memory_space=pl.ANY),
-            pl.BlockSpec(memory_space=pltpu.VMEM),
-            pl.BlockSpec(memory_space=pltpu.VMEM),
-        ],
-        out_specs=pl.BlockSpec(memory_space=pl.ANY),
+        in_specs=[pl.BlockSpec(memory_space=pltpu.HBM)] * 3,
+        out_specs=pl.BlockSpec(memory_space=pltpu.VMEM),
         scratch_shapes=[
+            pltpu.VMEM((2 * FREQS, SAMPLES), BF16),
+            pltpu.VMEM((2, 2, STATIONS), F32),
             pltpu.VMEM((2, HALF, HALF, SAMPLES), BF16),
             pltpu.VMEM((DEVS * ROWS_MSG, LANES), F32),
             pltpu.VMEM((DEVS, BANDS, TILES, BAND, LANES), BF16),
@@ -346,17 +343,16 @@
             pltpu.VMEM((DEVS, BANDS, TILES, BAND, LANES), BF16),
             pltpu.VMEM((DEVS, BANDS, TILES, BAND, LANES), BF16),
             pltpu.VMEM((BAND * 96, 2 * FREQS), BF16),
-            pltpu.VMEM((2, HALF, HALF, SAMPLES), BF16),
             pltpu.SMEM((2 * DEVS,), jnp.int32),
             pltpu.SemaphoreType.DMA((BANDS,)),
-            pltpu.SemaphoreType.DMA((BANDS,)),
+            pltpu.SemaphoreType.DMA((2,)),
             pltpu.SemaphoreType.DMA((6,)),
             pltpu.SemaphoreType.DMA((6,)),
         ],
         compiler_params=pltpu.CompilerParams(
-            collective_id=0, has_side_effects=True, vmem_limit_bytes=56 * 1024 * 1024
+            collective_id=0, has_side_effects=True, vmem_limit_bytes=46 * 1024 * 1024
         ),
-    )(halves, basis, source_weight)
+    )(halves, in_hbm(basis), in_hbm(source_weight))
     return series.reshape(2 * HALF, HALF, SAMPLES)
 
 

time: 129 us -> 124 us (0.961)
  Pallas kernels: 124 us -> 121 us
  local copies, waits for them, and re-layouts: 4.85 us -> 2.19 us
    pallas_call x1, Pallas kernels: 124 us -> 121 us  [on_device(): pl.pallas_call(predict_kernel, name='predict', out_shape=jax.ShapeDtypeSt...]
    unnamed x1, local copies, waits for them, and re-layouts: 4.85 us -> 2.19 us
where the time goes in v4:
time: 124 us; the launch traced here: 123 us
  Pallas kernels  121 us (98%)
  local copies, waits for them, and re-layouts  2.19 us (2%)
    pallas_call x1, Pallas kernels, on_device(): pl.pallas_call(predict_kernel, name='predict', out_shape=jax.ShapeDtypeSt...  121 us

profile of v4, /device:TPU:2, one launch (start us, length us, event | category | flops | bytes accessed | tf_op | source)
XLA Modules:
  0.0 123.4 jit_solution(13299204183401504702)
XLA Ops:
  0.0 121.2 %predict.1 = bf16[2,48,48,512]{3,2,1,0:T(8,128)(2,1)S(1)} custom-call(bf16[2,48,48,512]{3,2,1,0:T(8,128)(2,1)} %bitcast.3, bf16[512,512]{1,0:T(8,128)(2,1)} %constant.2.clone.basis_hbm, f32[2,2,768]{2,1,0:T(2,128)} %weight_hbm.1), custom_call_target="tpu_custom_call" | custom-call | tf_op jit(solution)/shard_map/predict/pallas_call | solution.py:326
  121.2 2.2 %copy.5 = bf16[96,48,512]{2,1,0:T(8,128)(2,1)} copy(bf16[96,48,512]{2,1,0:T(8,128)(2,1)S(1)} %bitcast.2) | data formatting | bytes 9437184

commit v5 on v4

--- a/solution.py
+++ b/solution.py
@@ -26,6 +26,16 @@
 ROWS_MSG = TILES * BAND
 
 
+STEPS = (
+    85, 84, 117, 116, 83, 52, 53, 77, 87, 92, 76, 93, 82, 86, 94, 10, 95, 11, 81, 4, 79, 27, 54,
+    99, 119, 34, 80, 5, 118, 35, 55, 98, 78, 26, 46, 121, 44, 120, 45, 122, 47, 123, 14, 89, 13,
+    88, 12, 91, 15, 90, 71, 17, 69, 16, 74, 30, 68, 19, 73, 31, 108, 57, 109, 56, 75, 29, 110,
+    59, 111, 58, 72, 28, 70, 18, 105, 39, 114, 38, 115, 61, 104, 60, 102, 41, 125, 40, 20, 64,
+    124, 50, 103, 51, 21, 65, 127, 43, 113, 36, 63, 106, 112, 37, 23, 67, 126, 42, 22, 66, 62,
+    107, 49, 100, 48, 101, 1, 32, 33, 6, 96, 97, 25, 2, 9, 24, 8, 7, 3,
+)
+
+
 def basis_table():
     freq = np.arange(FREQS)
     phase = ((freq[:, None] * np.arange(SAMPLES)[None, :]) % SAMPLES).astype(np.float32)
@@ -52,11 +62,9 @@
     zs = [2 * ((z + d) % 4) for d in range(4)]
     cs = [(c + d) % 2 for d in range(2)]
     order = []
-    for step in range(1, DEVS):
-        v = step * 63 % DEVS
-        bit = [(v >> b) & 1 for b in range(7)]
-        dx, dy, dz = 2 * bit[0] + bit[5], 2 * bit[1] + bit[2], 2 * bit[6] + bit[4]
-        order.append((zs[dz] + ys[dy][0], ys[dy][1] + xs[dx] + cs[bit[3]]))
+    for step in STEPS:
+        dx, dy, dz, dc = step // 32, step // 8 % 4, step // 2 % 4, step % 2
+        order.append((zs[dz] + ys[dy][0], ys[dy][1] + xs[dx] + cs[dc]))
     return order
 
 
@@ -192,7 +200,7 @@
                         mbuf[gl // 2, rows, pl.ds((jh * TILES + k) * LANES, LANES)] = out[k]
             return carry
 
-        lax.fori_loop(0, SHOTS * BANDS, step, 0)
+        lax.fori_loop(0, SHOTS * BANDS, step, 0, unroll=3)
 
     def average_and_weight(f):
         def block_row(bi, carry):
@@ -214,7 +222,7 @@
                 lbuf[here, pl.ds(2 * STATIONS + bj * LANES, LANES)] = li.astype(BF16)
             return carry
 
-        lax.fori_loop(0, STATIONS // LANES, block_row, 0)
+        lax.fori_loop(0, STATIONS // LANES, block_row, 0, unroll=6)
 
     def multiply():
         def columns(n, carry):
@@ -225,11 +233,11 @@
                 pbuf[c, :, cols] = jnp.dot(lhs, rhs, preferred_element_type=F32).astype(BF16)
             return carry
 
-        lax.fori_loop(0, STATIONS // 256, columns, 0)
-
-    def scatter(f):
+        lax.fori_loop(0, STATIONS // 256, columns, 0, unroll=3)
+
+    def scatter(f, low, high):
         def step(n, carry):
-            i, ts = n // BANDS, n % BANDS
+            i, ts = n % SHOTS, n // SHOTS
             for jh in range(2):
                 cut = []
                 for gl in range(4):
@@ -259,7 +267,7 @@
                         )
             return carry
 
-        lax.fori_loop(0, SHOTS * BANDS, step, 0)
+        lax.fori_loop(low * SHOTS, high * SHOTS, step, 0, unroll=4)
 
     def series(ts):
         flat_back = back.reshape(DEVS * BANDS * ROWS_MSG, LANES)
@@ -293,14 +301,15 @@
     assemble(0)
     average_and_weight(0)
     multiply()
-    scatter(0)
+    scatter(0, 0, BANDS)
     send_all(s2, back, 3, everything, pl.ds(0, 1))
     wait_recv(r1, 2, everything, pl.ds(2, 1))
     assemble(1)
     average_and_weight(1)
     multiply()
-    scatter(1)
+    scatter(1, 0, BANDS - 1)
     send_all(s2, back, 4, lead, pl.ds(1, 2))
+    scatter(1, BANDS - 1, BANDS)
     send_all(s2, back, 5, pl.ds(BANDS - 1, 1), pl.ds(1, 2))
     wait_send(s1, 0, first, pl.ds(0, 2))
     wait_send(s1, 1, later, pl.ds(0, 2))

time: 124 us -> 120 us (0.968); the launches traced: 123 us -> 118 us
  Pallas kernels: 121 us -> 115 us
    pallas_call x1, Pallas kernels: 121 us -> 115 us  [on_device(): pl.pallas_call(predict_kernel, name='predict', out_shape=jax.ShapeDtypeSt...]
where the time goes in v5:
time: 120 us; the launch traced here: 118 us
  Pallas kernels  115 us (96%)
  local copies, waits for them, and re-layouts  2.19 us (2%)
    pallas_call x1, Pallas kernels, on_device(): pl.pallas_call(predict_kernel, name='predict', out_shape=jax.ShapeDtypeSt...  115 us

profile of v5, /device:TPU:2, one launch (start us, length us, event | category | flops | bytes accessed | tf_op | source)
XLA Modules:
  0.0 117.5 jit_solution(10619763872063388263)
XLA Ops:
  0.0 115.3 %predict.1 = bf16[2,48,48,512]{3,2,1,0:T(8,128)(2,1)S(1)} custom-call(bf16[2,48,48,512]{3,2,1,0:T(8,128)(2,1)} %bitcast.3, bf16[512,512]{1,0:T(8,128)(2,1)} %constant.2.clone.basis_hbm, f32[2,2,768]{2,1,0:T(2,128)} %weight_hbm.1), custom_call_target="tpu_custom_call" | custom-call | tf_op jit(solution)/shard_map/predict/pallas_call | solution.py:335
  115.3 2.2 %copy.5 = bf16[96,48,512]{2,1,0:T(8,128)(2,1)} copy(bf16[96,48,512]{2,1,0:T(8,128)(2,1)S(1)} %bitcast.2) | data formatting | bytes 9437184

commit v6 on v5

--- a/solution.py
+++ b/solution.py
@@ -27,12 +27,12 @@
 
 
 STEPS = (
-    85, 84, 117, 116, 83, 52, 53, 77, 87, 92, 76, 93, 82, 86, 94, 10, 95, 11, 81, 4, 79, 27, 54,
-    99, 119, 34, 80, 5, 118, 35, 55, 98, 78, 26, 46, 121, 44, 120, 45, 122, 47, 123, 14, 89, 13,
-    88, 12, 91, 15, 90, 71, 17, 69, 16, 74, 30, 68, 19, 73, 31, 108, 57, 109, 56, 75, 29, 110,
-    59, 111, 58, 72, 28, 70, 18, 105, 39, 114, 38, 115, 61, 104, 60, 102, 41, 125, 40, 20, 64,
-    124, 50, 103, 51, 21, 65, 127, 43, 113, 36, 63, 106, 112, 37, 23, 67, 126, 42, 22, 66, 62,
-    107, 49, 100, 48, 101, 1, 32, 33, 6, 96, 97, 25, 2, 9, 24, 8, 7, 3,
+    85, 84, 86, 2, 87, 116, 34, 119, 52, 67, 118, 53, 66, 22, 77, 91, 83, 7, 92, 8, 82, 6, 76,
+    25, 93, 9, 117, 32, 1, 124, 40, 125, 41, 21, 65, 108, 24, 69, 17, 68, 16, 37, 113, 36, 112,
+    95, 10, 94, 3, 79, 26, 78, 27, 46, 122, 47, 123, 44, 121, 45, 120, 75, 31, 74, 30, 109, 33,
+    51, 102, 50, 103, 19, 71, 18, 70, 81, 5, 80, 4, 114, 39, 115, 38, 90, 15, 106, 62, 107, 63,
+    60, 105, 20, 64, 54, 99, 55, 98, 61, 104, 59, 110, 58, 111, 29, 72, 28, 73, 42, 127, 23, 35,
+    96, 12, 57, 97, 13, 56, 100, 48, 101, 49, 126, 43, 88, 11, 89, 14,
 )
 
 

time: 120 us -> 119 us (level)
  no operation moved by 1% of the time
where the time goes in v6:
time: 119 us; the launch traced here: 117 us
  Pallas kernels  115 us (97%)
  local copies, waits for them, and re-layouts  2.19 us (2%)
    pallas_call x1, Pallas kernels, on_device(): pl.pallas_call(predict_kernel, name='predict', out_shape=jax.ShapeDtypeSt...  115 us

profile of v6, /device:TPU:2, one launch (start us, length us, event | category | flops | bytes accessed | tf_op | source)
XLA Modules:
  0.0 116.9 jit_solution(5287533397501515910)
XLA Ops:
  0.0 114.7 %predict.1 = bf16[2,48,48,512]{3,2,1,0:T(8,128)(2,1)S(1)} custom-call(bf16[2,48,48,512]{3,2,1,0:T(8,128)(2,1)} %bitcast.3, bf16[512,512]{1,0:T(8,128)(2,1)} %constant.2.clone.basis_hbm, f32[2,2,768]{2,1,0:T(2,128)} %weight_hbm.1), custom_call_target="tpu_custom_call" | custom-call | tf_op jit(solution)/shard_map/predict/pallas_call | solution.py:335
  114.7 2.2 %copy.5 = bf16[96,48,512]{2,1,0:T(8,128)(2,1)} copy(bf16[96,48,512]{2,1,0:T(8,128)(2,1)S(1)} %bitcast.2) | data formatting | bytes 9437184
